TPU v7x, 128 devices: a whole 4x4x4 slice. The times are simulated.
128 devices in a mesh: lat: 32 (over y, x, core), chan: 4 (over z).
Axes of the slice: x: 4, y: 4, z: 4, core: 2. Of those that a mesh axis runs over, the one named last changes fastest.
Arguments:
- fields: float32 [1, 256, 12, 28800], P(None, 'lat', 'chan'), may hold values from -1000 to 1000
- cotangent: float32 [1, 256, 12, 28800], P(None, 'lat', 'chan'), may hold values from -6 to 6
- norm_gain: float32 [768], P('chan'), may hold values from 0.1 to 1.9
- norm_shift: float32 [768], P('chan'), may hold values from -3 to 3
- first_weight: float32 [2, 8, 9216], P(None, 'chan'), may hold values from -0.4375 to 0.4375
- first_bias: float32 [2, 8, 96], P(None, 'chan'), may hold values from -3 to 3
- second_weight: float32 [2, 8, 9216], P(None, 'chan'), may hold values from -0.4375 to 0.4375
- second_bias: float32 [2, 8, 96], P(None, 'chan'), may hold values from -3 to 3
Outputs:
- mixed_field: float32 [1, 256, 12, 28800], P(None, 'lat', 'chan')
- grad_fields: float32 [1, 256, 12, 28800], P(None, 'lat', 'chan')
- grad_gain: float32 [768], P('chan')
- grad_shift: float32 [768], P('chan')
- grad_first_weight: float32 [2, 8, 9216], P(None, 'chan')
- grad_first_bias: float32 [2, 8, 96], P(None, 'chan')
- grad_second_weight: float32 [2, 8, 9216], P(None, 'chan')
- grad_second_bias: float32 [2, 8, 96], P(None, 'chan')
All inputs are finite; a program needn't handle non-finite values.
Results may differ from a plain program's by a relative error of at most 0.0044.
Values sent between devices are 32-bit elements; how exact they have to be, the bound alone decides.
A program may use at most 128 MiB of HBM per device.

v0:
```python
import functools
import math

import jax
import jax.numpy as jnp
import ml_dtypes
import numpy as np
from jax import lax
from jax.experimental import pallas as pl
from jax.experimental.pallas import tpu as pltpu
from jax.sharding import PartitionSpec as P

F32 = jnp.float32
BF16 = jnp.bfloat16
MESH = pl.DeviceIdType.MESH

LON = 450
EMBED = 768
LOCAL = 192
BLOCK = 96
PAIRS = 225
PADDED = 240
STRIP = PADDED * 8
REAL = PAIRS * 8
RANK = 112
TALL = 120
OWN = 7
KINDS = 3
CHUNK = OWN * KINDS * 8
PIECE = 384
GRAD_ROWS = 104
PART = 32
PARTS = 4 * GRAD_ROWS // PART

epsilon = 1e-05
shrink_level = 0.05

SIX = ((1, 1), (0, 2), (2, 0), (0, 1), (1, 0), (0, 0))
THREE = ((0, 1), (1, 0), (0, 0))
FACTOR = 1.0 / math.sqrt(256 * LON)


def split_table(values, count):
    parts = []
    rest = values.astype(np.float64)
    for _ in range(count):
        part = rest.astype(np.float32).astype(ml_dtypes.bfloat16)
        parts.append(part)
        rest = rest - part.astype(np.float64)
    return np.stack(parts)


def make_tables():
    order = np.array([0] + list(range(2, 113)) + [1])
    places = np.arange(PAIRS)
    angles = 2.0 * np.pi * (order[:, None] * places[None, :] % PAIRS) / PAIRS
    plain = np.zeros((PADDED, PADDED))
    plain[: len(order), :PAIRS] = np.cos(angles) / np.sqrt(LON)
    plain[TALL : TALL + len(order), :PAIRS] = -np.sin(angles) / np.sqrt(LON)
    scale = np.full(TALL, 2.0)
    scale[0] = 1.0
    double = plain * np.concatenate([scale, scale])[:, None]
    turn = np.zeros((2, TALL, 128), np.float32)
    turn[0, :, :64] = 1.0
    turn[0, : len(order), 64:] = np.cos(2.0 * np.pi * order / LON)[:, None]
    turn[1, : len(order), 64:] = np.sin(2.0 * np.pi * order / LON)[:, None]
    rows = np.arange(256)
    lat_angles = 2.0 * np.pi * (rows[:, None] * rows[None, :] % 256) / 256
    lat = np.concatenate([np.cos(lat_angles), np.sin(lat_angles)]) / 16.0
    place = np.zeros((2, 2, 2, 128, 256), np.float32)
    for core in range(2):
        for mode in range(2):
            for part in range(2):
                for i in range(BLOCK):
                    in_shared = i >= 64 if core == 0 else i < 32
                    if in_shared:
                        lane = 128 + 64 * part + 32 * mode + i % 32
                    else:
                        lane = 64 * part + (i if core == 0 else i - 32)
                    place[core, mode, part, i, lane] = 1.0
    halves = np.zeros((2, 8, 128), np.float32)
    halves[0, 0, :64] = 1.0
    halves[0, 1, 64:] = 1.0
    halves[1, 2, :64] = 1.0
    halves[1, 3, 64:] = 1.0
    bf = ml_dtypes.bfloat16
    return (
        split_table(plain, 3),
        split_table(double, 2),
        split_table(plain.T, 2),
        split_table(double.T, 2),
        split_table(lat, 3),
        turn,
        place.astype(bf),
        np.swapaxes(place, -1, -2).astype(bf),
        halves,
    )


def split(value, count):
    parts = []
    for _ in range(count):
        part = value.astype(BF16)
        parts.append(part)
        value = value - part.astype(F32)
    return parts


def dots(left, right, pairs, dims=((1,), (0,))):
    total = None
    for i, j in pairs:
        term = lax.dot_general(left[i], right[j], (dims, ((), ())), preferred_element_type=F32)
        total = term if total is None else total + term
    return total


def kernel(
    fields,
    cotangent,
    norm,
    weights,
    plain,
    double,
    back_plain,
    back_double,
    lat_table,
    turn,
    place,
    place_t,
    halves,
    mixed_out,
    grad_out,
    param_out,
    norm_out,
    scaled,
    cot,
    inv,
    result,
    send1,
    send2,
    send3,
    send4,
    recv1,
    recv2,
    recv3,
    recv4,
    mid1,
    mid2,
    mid3,
    mid4,
    act,
    shrunk,
    mats,
    mats_grad,
    sums_grad,
    bias,
    zsend,
    zrecv,
    part_send,
    part_recv,
    part_sum,
    norm_send,
    norm_recv,
    io_sem,
    z_ssem,
    z_rsem,
    s_sem,
    r_sem,
    m_sem,
    p_ssem,
    p_rsem,
    g_ssem,
    g_rsem,
    n_ssem,
    n_rsem,
):
    me = lax.axis_index("lat")
    zed = lax.axis_index("chan")
    y, x, core = me // 8, (me // 2) % 4, me % 2
    chip = y * 4 + x
    lane = lax.broadcasted_iota(jnp.int32, (1, 128), 1)
    low = lane < 64
    low32 = lane % 64 < 32
    sign = jnp.where(low, 1.0, -1.0).astype(F32)

    sends = (send1, send2, send3, send4)
    recvs = (recv1, recv2, recv3, recv4)
    mids = (mid1, mid2, mid3, mid4)

    def at(dy, dx):
        return lax.rem(y + dy, 4), lax.rem(x + dx, 4)

    def index(row, column, half):
        return (row * 4 + column) * 2 + half

    def row_slot(row, column, half):
        return half * 16 + row * 4 + column

    def slots(n):
        return (row_slot, index) if n < 2 else (index, row_slot)

    direct = [(0, 0, 2)] + [(0, d, k) for d in (1, 3, 2) for k in (0, 1)]
    direct += [(d, 0, k) for d in (1, 3, 2) for k in (0, 1)]
    corner = [(dy, dx, k) for dy in (1, 3, 2) for dx in (1, 3, 2) for k in (0, 1)]

    def corner_slot(dy, dx, k):
        return k * 9 + (dy - 1) * 3 + dx - 1

    def remote(src, dst, ssem, rsem, device):
        return pltpu.make_async_remote_copy(
            src_ref=src,
            dst_ref=dst,
            send_sem=ssem,
            recv_sem=rsem,
            device_id=(device, zed),
            device_id_type=MESH,
        )

    def first_leg(n, i):
        dy, dx, k = corner[i]
        row, column = at(dy, dx)
        src_slot = slots(n)[0](row, column, k)
        slot = corner_slot(dy, dx, k)
        device = index(y, column, core) if k == 0 else index(row, x, core)
        return remote(
            sends[n].at[src_slot], mids[n].at[slot], s_sem.at[n, i], m_sem.at[n, slot], device
        )

    def second_leg(n, i):
        dy, dx, k = corner[i]
        slot = corner_slot(dy, dx, k)
        if k == 0:
            origin = (y, lax.rem(x + 4 - dx, 4))
            final = (lax.rem(y + dy, 4), x)
        else:
            origin = (lax.rem(y + 4 - dy, 4), x)
            final = (y, lax.rem(x + dx, 4))
        return remote(
            mids[n].at[slot],
            recvs[n].at[slots(n)[1](origin[0], origin[1], core)],
            s_sem.at[n, 18 + i],
            r_sem.at[n, index(origin[0], origin[1], core)],
            index(final[0], final[1], k),
        )

    def direct_leg(n, i):
        dy, dx, k = direct[i]
        half = 1 - core if k == 2 else k
        row, column = at(dy, dx)
        return remote(
            sends[n].at[slots(n)[0](row, column, half)],
            recvs[n].at[slots(n)[1](y, x, core)],
            s_sem.at[n, 36 + i],
            r_sem.at[n, me],
            index(row, column, half),
        )

    def start(n):
        for i in range(18):
            first_leg(n, i).start()
        for i in range(13):
            direct_leg(n, i).start()
        mine = slots(n)[0](y, x, core)
        theirs = slots(n)[1](y, x, core)
        recvs[n][theirs] = sends[n][mine]

    def forward(n):
        for i in range(18):
            first_leg(n, i).wait_recv()
            second_leg(n, i).start()

    def finish(n):
        for d in range(1, 32):
            origin = lax.rem(me + d, 32)
            slot = slots(n)[1](origin // 8, (origin // 2) % 4, origin % 2)
            remote(
                sends[n].at[0], recvs[n].at[slot], s_sem.at[n, 0], r_sem.at[n, origin], origin
            ).wait_recv()

    def drain(n):
        for i in range(18):
            first_leg(n, i).wait_send()
            second_leg(n, i).wait_send()
        for i in range(13):
            direct_leg(n, i).wait_send()

    def exchange(stage):
        copies = []
        for d in range(1, 4):
            other = lax.rem(zed + d, 4)
            copies.append(
                pltpu.make_async_remote_copy(
                    src_ref=zsend.at[stage],
                    dst_ref=zrecv.at[stage, zed],
                    send_sem=z_ssem.at[stage, d],
                    recv_sem=z_rsem.at[stage, zed],
                    device_id=(me, other),
                    device_id_type=MESH,
                )
            )
        for copy in copies:
            copy.start()
        zrecv[stage, zed] = zsend[stage]
        return copies

    def exchange_wait(stage, copies):
        for copy in copies:
            copy.wait_send()
        for d in range(1, 4):
            other = lax.rem(zed + d, 4)
            pltpu.make_async_remote_copy(
                src_ref=zsend.at[stage],
                dst_ref=zrecv.at[stage, other],
                send_sem=z_ssem.at[stage, d],
                recv_sem=z_rsem.at[stage, other],
                device_id=(me, other),
                device_id_type=MESH,
            ).wait_recv()

    def token_sums(value, which, count=3):
        pattern = halves[which].astype(BF16)
        total = None
        for part in reversed(split(value, count)):
            term = lax.dot_general(
                pattern, part, (((1,), (1,)), ((), ())), preferred_element_type=F32
            )
            total = term if total is None else total + term
        return total

    def spread(rows, which):
        return lax.dot_general(
            rows,
            halves[which],
            (((0,), (0,)), ((), ())),
            precision=lax.Precision.HIGHEST,
            preferred_element_type=F32,
        )

    def lon_forward(load, table, pairs, out):
        count = 3 if pairs is SIX else 2
        flat = out.reshape(32 * CHUNK, 128)
        cos_turn, sin_turn = turn[0], turn[1]
        top = lax.broadcasted_iota(jnp.int32, (TALL, 128), 0) == 0
        for g in range(3):

            def body(step, carry, g=g):
                h0 = step * 2
                data = jnp.concatenate([load(g, h0), load(g, h0 + 1)], axis=1)
                parts = split(data, count)
                both = dots([table[i] for i in range(count)], parts, pairs)
                for e in range(2):
                    real = both[:TALL, 128 * e : 128 * e + 128]
                    imag = both[TALL:, 128 * e : 128 * e + 128]
                    turned_real = real * cos_turn + imag * sin_turn
                    turned_imag = imag * cos_turn - real * sin_turn
                    even = jnp.where(low, turned_real, pltpu.roll(turned_imag, 64, 1))
                    odd = jnp.where(low, pltpu.roll(turned_real, 64, 1), turned_imag)
                    a = even + odd
                    b = (even - odd) * sign
                    b = jnp.where(top, a[RANK : RANK + 1], b)
                    h = h0 + e

                    def store(half, kind, value):
                        flat[pl.ds(half * 16 * CHUNK + kind * 8 + h, RANK, stride=24), :] = value[
                            :RANK
                        ]

                    if g == 1:
                        store(0, 2, jnp.where(low32, a, pltpu.roll(b, 32, 1)))
                        store(1, 2, jnp.where(low32, pltpu.roll(a, 96, 1), b))
                    else:
                        store(g // 2, 0, a)
                        store(g // 2, 1, b)
                return carry

            lax.fori_loop(0, 4, body, 0)

    def lon_inverse(source, table):
        flat = source.reshape(32 * CHUNK, 128)
        cos_turn, sin_turn = turn[0], turn[1]
        top = lax.broadcasted_iota(jnp.int32, (RANK, 128), 0) == 0
        top8 = lax.broadcasted_iota(jnp.int32, (8, 128), 0) == 0
        for g in range(3):

            def body(step, carry, g=g):
                h0 = step * 2
                columns = []
                for e in range(2):
                    h = h0 + e

                    def fetch(half, kind):
                        return flat[pl.ds(half * 16 * CHUNK + kind * 8 + h, RANK, stride=24), :]

                    if g == 1:
                        u0, u1 = fetch(0, 2), fetch(1, 2)
                        a = jnp.where(low32, u0, pltpu.roll(u1, 32, 1))
                        b = jnp.where(low32, pltpu.roll(u0, 96, 1), u1)
                    else:
                        a, b = fetch(g // 2, 0), fetch(g // 2, 1)
                    last = jnp.where(top8, b[0:1], 0.0)
                    b = jnp.where(top, 0.0, b * sign)
                    even = jnp.concatenate([a + b, last], axis=0)
                    odd = jnp.concatenate([a - b, last], axis=0)
                    real = jnp.where(low, even, pltpu.roll(odd, 64, 1))
                    imag = jnp.where(low, pltpu.roll(even, 64, 1), odd)
                    turned_real = real * cos_turn - imag * sin_turn
                    turned_imag = imag * cos_turn + real * sin_turn
                    columns.append(jnp.concatenate([turned_real, turned_imag], axis=0))
                data = jnp.concatenate(columns, axis=1)
                out = dots([table[0], table[1]], split(data, 2), THREE)
                for e in range(2):
                    result[pl.ds(g * STRIP + h0 + e, PADDED, stride=8), :] = out[
                        :, 128 * e : 128 * e + 128
                    ]
                return carry

            lax.fori_loop(0, 4, body, 0)

    def piece(ref, r, kind):
        return ref[:, pl.ds(pl.multiple_of(r * 24 + kind * 8, 8), 8), :].reshape(256, 128)

    def put(ref, r, kind, value):
        ref[:, pl.ds(pl.multiple_of(r * 24 + kind * 8, 8), 8), :] = value.reshape(32, 8, 128)

    def lat_mix(pieces, orient, pairs):
        count = 3 if pairs is SIX else 2
        data = jnp.concatenate(pieces, axis=1)
        both = dots([lat_table[i] for i in range(count)], split(data, count), pairs)
        out = []
        for kind in range(3):
            direct_part = both[:256, 128 * kind : 128 * kind + 128]
            turned = both[256:, 128 * kind : 128 * kind + 128]
            out.append(direct_part + (orient * sign) * pltpu.roll(turned, 64, 1))
        return out

    def apply(pieces, layer, pairs, transposed):
        count = 3 if pairs is SIX else 2
        dims = ((1,), (1,)) if transposed else ((1,), (0,))
        parts = [split(value, count) for value in pieces]
        out = []
        for mode in range(2):
            left = [
                jnp.concatenate([parts[mode][i], parts[2][i]], axis=1) for i in range(count)
            ]
            right = [mats[layer * 2 + mode, i] for i in range(count)]
            out.append(dots(left, right, pairs, dims))
        return [out[0][:, :128], out[1][:, :128], out[0][:, 128:] + out[1][:, 128:]]

    def mat_grad(inputs, outputs, layer):
        left = [split(value, 2) for value in inputs]
        right = [split(value, 2) for value in outputs]
        for mode in range(2):
            lhs = [jnp.concatenate([left[mode][i], left[2][i]], axis=1) for i in range(2)]
            rhs = [jnp.concatenate([right[mode][i], right[2][i]], axis=1) for i in range(2)]
            mats_grad[layer * 2 + mode] += dots(lhs, rhs, THREE, ((0,), (0,)))
            total = jnp.concatenate([outputs[mode], outputs[2]], axis=1)
            sums_grad[layer * 2 + mode] += jnp.sum(total.reshape(32, 8, 256), axis=0)

    loads = []
    for g in range(3):
        loads.append(
            pltpu.make_async_copy(
                cotangent.at[g], cot.at[pl.ds(g * STRIP, REAL)], io_sem.at[g]
            )
        )
    for g in range(3):
        loads.append(
            pltpu.make_async_copy(
                fields.at[g], scaled.at[pl.ds(g * STRIP, REAL)], io_sem.at[3 + g]
            )
        )
    for copy in loads:
        copy.start()
    barrier = pltpu.get_barrier_semaphore()
    for d in range(1, 32):
        pl.semaphore_signal(
            barrier, inc=1, device_id=(lax.rem(me + d, 32), zed), device_id_type=MESH
        )
    for d in range(1, 4):
        pl.semaphore_signal(
            barrier, inc=1, device_id=(me, lax.rem(zed + d, 4)), device_id_type=MESH
        )
    for g in range(3):
        cot[pl.ds(g * STRIP + REAL, STRIP - REAL), :] = jnp.zeros((STRIP - REAL, 128), F32)
        scaled[pl.ds(g * STRIP + REAL, STRIP - REAL), :] = jnp.zeros((STRIP - REAL, 128), F32)
    for copy in loads[:3]:
        copy.wait()

    def load_cot(g, h):
        return cot[pl.ds(g * STRIP + h, PADDED, stride=8), :]

    lon_forward(load_cot, double, THREE, send2)
    pl.semaphore_wait(barrier, 34)
    start(1)

    for copy in loads[3:]:
        copy.wait()
    for k in range(STRIP // PIECE):
        rows = [scaled[pl.ds(g * STRIP + k * PIECE, PIECE), :] for g in range(3)]
        here = token_sums(rows[0] + rows[1] + rows[2], 0)
        mean = spread(here * (1.0 / LOCAL), 0)
        square = None
        for value in rows:
            centred = value - mean
            square = centred * centred if square is None else square + centred * centred
        zsend[0, :, pl.ds(k * PIECE, PIECE)] = here + token_sums(square, 1)
    copies = exchange(0)
    exchange_wait(0, copies)
    row8 = lax.broadcasted_iota(jnp.int32, (8, PIECE), 0)
    for k in range(STRIP // PIECE):
        group = [zrecv[0, i, :, pl.ds(k * PIECE, PIECE)] for i in range(4)]
        total = (group[0] + group[1]) + (group[2] + group[3])
        mean = total * (1.0 / EMBED)
        apart = None
        for value in group:
            gap = value * (1.0 / LOCAL) - mean
            apart = gap * gap if apart is None else apart + gap * gap
        variance = (total + pltpu.roll(apart, 2, 0) * LOCAL) * (1.0 / EMBED)
        both = jnp.where(row8 < 2, mean, lax.rsqrt(jnp.maximum(variance, 0.0) + epsilon))
        mean = spread(both, 0)
        inverse = spread(both, 1)
        inv[pl.ds(k * PIECE, PIECE), :] = inverse
        for g in range(3):
            here = pl.ds(g * STRIP + k * PIECE, PIECE)
            scaled[here, :] = (scaled[here, :] - mean) * inverse

    def load_normed(g, h):
        value = scaled[pl.ds(g * STRIP + h, PADDED, stride=8), :]
        return value * norm[g : g + 1] + norm[3 + g : 4 + g]

    lon_forward(load_normed, plain, SIX, send1)
    start(0)
    forward(1)

    for layer in range(2):
        for mode in range(2):
            to_real, to_imag = place[core, mode, 0], place[core, mode, 1]
            real = split(weights[layer, 0, core], 3)
            imag = split(weights[layer, 1, core], 3)

            def fan(parts, target):
                total = None
                for part in reversed(parts):
                    term = jnp.dot(part, target, preferred_element_type=F32)
                    total = term if total is None else total + term
                return total

            upper = fan(real, to_real) + fan(imag, to_imag)
            lower = fan(real, to_imag) - fan(imag, to_real)
            bias[layer * 2 + mode] = jnp.broadcast_to(upper[BLOCK : BLOCK + 1], (8, 256))

            def lift(source, value):
                total = None
                for part in reversed(split(value, 3)):
                    term = jnp.dot(source, part, preferred_element_type=F32)
                    total = term if total is None else total + term
                return total

            whole = lift(place_t[core, mode, 0], upper) + lift(place_t[core, mode, 1], lower)
            for i, part in enumerate(split(whole, 3)):
                mats[layer * 2 + mode, i] = part

    def add_bias(pieces, layer):
        first, second = bias[layer * 2], bias[layer * 2 + 1]
        return [
            pieces[0] + first[0:1, :128],
            pieces[1] + second[0:1, :128],
            pieces[2] + (first[0:1, 128:] + second[0:1, 128:]),
        ]

    finish(1)

    def upstream_body(r, carry):
        out = lat_mix([piece(recv2, r, kind) for kind in range(3)], 1.0, THREE)
        for kind in range(3):
            put(recv2, r, kind, out[kind])
        return carry

    lax.fori_loop(0, OWN, upstream_body, 0)
    forward(0)
    finish(0)

    def forward_body(r, carry):
        spectrum = lat_mix([piece(recv1, r, kind) for kind in range(3)], 1.0, SIX)
        for kind in range(3):
            put(recv1, r, kind, spectrum[kind])
        hidden = [jnp.maximum(v, 0.0) for v in add_bias(apply(spectrum, 0, SIX, False), 0)]
        for kind in range(3):
            put(act, r, kind, hidden[kind])
        out = add_bias(apply(hidden, 1, SIX, False), 1)
        out = [v - jnp.clip(v, -shrink_level, shrink_level) for v in out]
        for kind in range(3):
            put(shrunk, r, kind, out[kind])
        rows = lat_mix(out, -1.0, THREE)
        for kind in range(3):
            put(send3, r, kind, rows[kind])
        return carry

    lax.fori_loop(0, OWN, forward_body, 0)
    start(2)

    mats_grad[...] = jnp.zeros_like(mats_grad)
    sums_grad[...] = jnp.zeros_like(sums_grad)

    def backward_body(r, carry):
        out_grad = [
            jnp.where(piece(shrunk, r, kind) != 0.0, piece(recv2, r, kind), 0.0)
            for kind in range(3)
        ]
        hidden = [piece(act, r, kind) for kind in range(3)]
        mat_grad(hidden, out_grad, 1)
        hidden_grad = apply(out_grad, 1, THREE, True)
        pre_grad = [jnp.where(h > 0.0, g, 0.0) for h, g in zip(hidden, hidden_grad)]
        mat_grad([piece(recv1, r, kind) for kind in range(3)], pre_grad, 0)
        rows = lat_mix(apply(pre_grad, 0, THREE, True), -1.0, THREE)
        for kind in range(3):
            put(send4, r, kind, rows[kind])
        return carry

    lax.fori_loop(0, OWN, backward_body, 0)

    bias_row = lax.broadcasted_iota(jnp.int32, (128, 128), 0) == BLOCK
    for layer in range(2):
        real_total, imag_total = None, None
        for mode in range(2):
            real_t, imag_t = place_t[core, mode, 0], place_t[core, mode, 1]
            real_p, imag_p = place[core, mode, 0], place[core, mode, 1]
            grads = split(mats_grad[layer * 2 + mode], 2)
            to_real = sum(jnp.dot(v, real_t, preferred_element_type=F32) for v in grads)
            to_imag = sum(jnp.dot(v, imag_t, preferred_element_type=F32) for v in grads)

            def lower_to(target, value):
                return sum(
                    jnp.dot(target, v, preferred_element_type=F32) for v in split(value, 2)
                )

            real = lower_to(real_p, to_real) + lower_to(imag_p, to_imag)
            imag = lower_to(real_p, to_imag) - lower_to(imag_p, to_real)
            column = jnp.sum(sums_grad[layer * 2 + mode], axis=0, keepdims=True)
            column = jnp.broadcast_to(column, (16, 256))
            sums = split(column, 3)
            real_bias = sum(jnp.dot(v, real_t, preferred_element_type=F32) for v in sums)
            imag_bias = sum(jnp.dot(v, imag_t, preferred_element_type=F32) for v in sums)
            real = jnp.where(bias_row, real_bias[0:1], real)
            imag = jnp.where(bias_row, imag_bias[0:1], imag)
            real_total = real if real_total is None else real_total + real
            imag_total = imag if imag_total is None else imag_total + imag
        part_send[pl.ds(layer * 2 * GRAD_ROWS, GRAD_ROWS), :] = real_total[:GRAD_ROWS]
        part_send[pl.ds((layer * 2 + 1) * GRAD_ROWS, GRAD_ROWS), :] = imag_total[:GRAD_ROWS]

    def part_copy(d):
        other = lax.rem(chip + d, 16)
        return other, remote(
            part_send.at[pl.ds(lax.rem(other, PARTS) * PART, PART)],
            part_recv.at[chip],
            p_ssem.at[d],
            p_rsem.at[chip],
            other * 2 + core,
        )

    for d in range(1, 16):
        other, copy = part_copy(d)
        pl.when(other < PARTS)(copy.start)
    part_recv[chip] = part_send[pl.ds(lax.rem(chip, PARTS) * PART, PART), :]
    start(3)
    forward(2)

    owner = chip < PARTS

    def sum_copy(d):
        other = lax.rem(me + d, 32)
        return other, remote(
            part_sum,
            param_out.at[core, pl.ds(lax.rem(chip, PARTS) * PART, PART)],
            g_ssem.at[d],
            g_rsem.at[me],
            other,
        )

    @pl.when(owner)
    def _():
        for d in range(1, 16):
            other = lax.rem(chip + d, 16)
            remote(
                part_send.at[pl.ds(0, PART)],
                part_recv.at[other],
                p_ssem.at[d],
                p_rsem.at[other],
                other * 2 + core,
            ).wait_recv()
        total = part_recv[0]
        for i in range(1, 16):
            total = total + part_recv[i]
        part_sum[...] = total * FACTOR
        param_out[core, pl.ds(lax.rem(chip, PARTS) * PART, PART), :] = total * FACTOR
        for d in range(1, 32):
            sum_copy(d)[1].start()

    finish(2)
    lon_inverse(recv3, back_double)
    for g in range(3):
        here = pl.ds(g * STRIP, REAL)
        result[here, :] = (
            result[here, :] + scaled[here, :] * norm[g : g + 1] + norm[3 + g : 4 + g]
        )
    stores = []
    for g in range(3):
        stores.append(
            pltpu.make_async_copy(
                result.at[pl.ds(g * STRIP, REAL)], mixed_out.at[g], io_sem.at[g]
            )
        )
        stores[-1].start()
    forward(3)
    for copy in stores:
        copy.wait()
    finish(3)

    lon_inverse(recv4, back_plain)
    gains = [None] * 6
    for k in range(STRIP // PIECE):
        direct_sum, cross_sum = None, None
        for g in range(3):
            here = pl.ds(g * STRIP + k * PIECE, PIECE)
            normed_grad = cot[here, :] + result[here, :]
            unit = scaled[here, :]
            for slot, value in ((g, normed_grad * unit), (3 + g, normed_grad)):
                value = jnp.sum(value.reshape(PIECE // 8, 8, 128), axis=0)
                gains[slot] = value if gains[slot] is None else gains[slot] + value
            scaled_grad = normed_grad * norm[g : g + 1]
            cot[here, :] = scaled_grad
            cross = scaled_grad * unit
            direct_sum = scaled_grad if direct_sum is None else direct_sum + scaled_grad
            cross_sum = cross if cross_sum is None else cross_sum + cross
        zsend[1, :, pl.ds(k * PIECE, PIECE)] = token_sums(direct_sum, 0) + token_sums(
            cross_sum, 1
        )
    copies = exchange(1)
    norm_rows = lax.broadcasted_iota(jnp.int32, (8, 128), 0)
    packed = jnp.zeros((8, 128), F32)
    for i, value in enumerate(gains):
        value = jnp.sum(value, axis=0, keepdims=True)
        packed = jnp.where(norm_rows == i, value, packed)
    norm_send[...] = packed + pltpu.roll(packed, 64, 1)
    norm_recv[me] = norm_send[...]

    def norm_copy(d):
        other = lax.rem(me + d, 32)
        return remote(norm_send, norm_recv.at[me], n_ssem.at[d], n_rsem.at[me], other)

    for d in range(1, 32):
        norm_copy(d).start()
    exchange_wait(1, copies)
    for k in range(STRIP // PIECE):
        group = [zrecv[1, i, :, pl.ds(k * PIECE, PIECE)] for i in range(4)]
        total = ((group[0] + group[1]) + (group[2] + group[3])) * (1.0 / EMBED)
        direct_mean = spread(total, 0)
        cross_mean = spread(total, 1)
        inverse = inv[pl.ds(k * PIECE, PIECE), :]
        for g in range(3):
            here = pl.ds(g * STRIP + k * PIECE, PIECE)
            cot[here, :] = inverse * (cot[here, :] - direct_mean - scaled[here, :] * cross_mean)
    stores = []
    for g in range(3):
        stores.append(
            pltpu.make_async_copy(
                cot.at[pl.ds(g * STRIP, REAL)], grad_out.at[g], io_sem.at[3 + g]
            )
        )
        stores[-1].start()

    for d in range(1, 32):
        other = lax.rem(me + d, 32)
        remote(
            norm_send, norm_recv.at[other], n_ssem.at[d], n_rsem.at[other], other
        ).wait_recv()
        norm_copy(d).wait_send()
    total = norm_recv[0]
    for i in range(1, 32):
        total = total + norm_recv[i]
    norm_out[...] = total * FACTOR
    for d in range(1, 16):
        other, copy = part_copy(d)
        pl.when(other < PARTS)(copy.wait_send)

    @pl.when(owner)
    def _():
        for d in range(1, 32):
            sum_copy(d)[1].wait_send()

    for d in range(1, 32):
        other = lax.rem(me + d, 32)
        other_chip = other // 2
        copy = remote(
            part_sum,
            param_out.at[other % 2, pl.ds(lax.rem(other_chip, PARTS) * PART, PART)],
            g_ssem.at[d],
            g_rsem.at[other],
            other,
        )
        pl.when(other_chip < PARTS)(copy.wait_recv)
    for n in range(4):
        drain(n)
    for copy in stores:
        copy.wait()


def shards(
    fields, cotangent, norm_gain, norm_shift, first_weight, first_bias, second_weight, second_bias
):
    def rows(values):
        return values.reshape(8, 3, PAIRS, 128).transpose(1, 2, 0, 3).reshape(3, REAL, 128)

    def unrows(values):
        return values.reshape(3, PAIRS, 8, 128).transpose(2, 0, 1, 3).reshape(1, 8, 3, LON * 64)

    norm = jnp.concatenate([norm_gain.reshape(3, 64), norm_shift.reshape(3, 64)])
    norm = jnp.pad(jnp.concatenate([norm, norm], axis=1), ((0, 2), (0, 0)))
    square = (2, 2, BLOCK, BLOCK)
    weights = jnp.stack([first_weight.reshape(square), second_weight.reshape(square)])
    biases = jnp.stack([first_bias, second_bias])[:, :, :, None, :]
    weights = jnp.concatenate([weights, biases], axis=3)
    weights = jnp.pad(weights, ((0, 0),) * 3 + ((0, 128 - BLOCK - 1), (0, 128 - BLOCK)))
    tables = make_tables()
    buffer = pltpu.VMEM((32, CHUNK, 128), F32)
    middle = pltpu.VMEM((18, CHUNK, 128), F32)
    strips = pltpu.VMEM((3 * STRIP, 128), F32)
    dma = pltpu.SemaphoreType.DMA
    vmem = pl.BlockSpec(memory_space=pltpu.VMEM)
    anywhere = pl.BlockSpec(memory_space=pl.ANY)
    mixed, grad, params, norms = pl.pallas_call(
        kernel,
        out_shape=(
            jax.ShapeDtypeStruct((3, REAL, 128), F32),
            jax.ShapeDtypeStruct((3, REAL, 128), F32),
            jax.ShapeDtypeStruct((2, 4 * GRAD_ROWS, 128), F32),
            jax.ShapeDtypeStruct((8, 128), F32),
        ),
        in_specs=[anywhere] * 2 + [vmem] * 11,
        out_specs=[anywhere] * 2 + [vmem] * 2,
        scratch_shapes=[
            strips,
            strips,
            pltpu.VMEM((STRIP, 128), F32),
            strips,
        ]
        + [buffer] * 8
        + [middle] * 4
        + [
            buffer,
            buffer,
            pltpu.VMEM((4, 3, 256, 256), BF16),
            pltpu.VMEM((4, 256, 256), F32),
            pltpu.VMEM((4, 8, 256), F32),
            pltpu.VMEM((4, 8, 256), F32),
            pltpu.VMEM((2, 8, STRIP), F32),
            pltpu.VMEM((2, 4, 8, STRIP), F32),
            pltpu.VMEM((4 * GRAD_ROWS, 128), F32),
            pltpu.VMEM((16, PART, 128), F32),
            pltpu.VMEM((PART, 128), F32),
            pltpu.VMEM((8, 128), F32),
            pltpu.VMEM((32, 8, 128), F32),
            dma((6,)),
            dma((2, 4)),
            dma((2, 4)),
            dma((4, 49)),
            dma((4, 32)),
            dma((4, 18)),
            dma((16,)),
            dma((16,)),
            dma((32,)),
            dma((32,)),
            dma((32,)),
            dma((32,)),
        ],
        compiler_params=pltpu.CompilerParams(
            collective_id=1, has_side_effects=True, vmem_limit_bytes=63 * 2**20
        ),
        cost_estimate=pl.CostEstimate(
            flops=5_500_000_000, bytes_accessed=12_000_000, transcendentals=0
        ),
        name="mixer",
    )(rows(fields), rows(cotangent), norm, weights, *tables)
    params = params.reshape(2, 2, 2, GRAD_ROWS, 128)[..., :BLOCK].transpose(1, 2, 0, 3, 4)
    flat = (2, 2, BLOCK * BLOCK)
    return (
        unrows(mixed),
        unrows(grad),
        norms[0:3, :64].reshape(LOCAL),
        norms[3:6, :64].reshape(LOCAL),
        params[0, :, :, :BLOCK].reshape(flat),
        params[0, :, :, BLOCK],
        params[1, :, :, :BLOCK].reshape(flat),
        params[1, :, :, BLOCK],
    )


def solution(mesh):
    big = P(None, "lat", "chan", None)
    small = P(None, "chan", None)
    return jax.shard_map(
        shards,
        mesh=mesh,
        in_specs=(big, big, P("chan"), P("chan"), small, small, small, small),
        out_specs=(big, big, P("chan"), P("chan"), small, small, small, small),
        check_vma=False,
    )
```

profile of v0, /device:TPU:1, one launch (start us, length us, event | category | flops | bytes accessed | tf_op | source)
XLA Modules:
  0.0 215.0 jit_solution(15068709656835896704)
XLA Ops:
  0.6 1.1 stack_reshape.6
  1.7 1.1 stack_reshape.7
  2.8 0.7 pad_maximum_fusion
  3.5 0.9 select_maximum_fusion.weights
  4.4 0.8 reshape.59
  5.1 0.8 reshape.60
  5.9 0.7 fusion.norm
  6.6 195.5 %mixer.1 = (f32[3,1800,128]{2,1,0:T(8,128)}, f32[3,1800,128]{2,1,0:T(8,128)}, f32[2,416,128]{2,1,0:T(8,128)}, f32[8,128]{1,0:T(8,128)}) custom-call(f32[3,1800,128]{2,1,0:T(8,128)} %bitcast.44, f32[3,1800,128]{2,1,0:T(8,128)} %bitcast.45, f32[8,128]{1,0:T(8,128)} %fusion.norm, f32[2,2,2,128,128]{4,3,2,1,0:T(8,128)} %select_maximum_fusion.weights, ...), custom_call_target="tpu_custom_call" | custom-call | flops 5500000256 | bytes 12000000 | tf_op jit(solution)/shard_map/mixer/pallas_call | solution.py:831
  202.1 0.0 copy-start.2
  202.1 0.0 copy-start.1
  202.1 1.5 copy.31
  203.6 0.1 fusion.1
  203.7 0.7 copy.27
  204.4 1.8 reshape_squeeze.6
  206.2 0.7 copy.28
  206.9 1.8 reshape_squeeze.7
  208.8 0.6 slice_bitcast_fusion
  209.3 0.0 copy-done.2
  209.4 0.6 reshape.65
  210.0 0.6 reshape.66
  210.6 0.0 copy-done.1
  210.6 0.0 copy-start
  210.6 1.5 copy.34
  212.2 1.2 copy-done
  213.4 1.5 copy.35
  (1 shorter events, 0.0 us)
Async XLA Ops:
  202.1 7.3 %copy-start.2 = (f32[8,128]{1,0:T(8,128)S(1)}, f32[8,128]{1,0:T(8,128)}, u32[]{:S(2)}) copy-start(f32[8,128]{1,0:T(8,128)} %get-tuple-element.14) | copy-start | bytes 12292
  202.1 8.6 %copy-start.1 = (f32[3,1800,128]{2,1,0:T(8,128)S(1)}, f32[3,1800,128]{2,1,0:T(8,128)}, u32[]{:S(2)}) copy-start(f32[3,1800,128]{2,1,0:T(8,128)} %get-tuple-element.12) | copy-start | bytes 8294404
  210.6 2.8 %copy-start = (f32[3,1800,128]{2,1,0:T(8,128)S(1)}, f32[3,1800,128]{2,1,0:T(8,128)}, u32[]{:S(2)}) copy-start(f32[3,1800,128]{2,1,0:T(8,128)} %get-tuple-element.13) | copy-start | bytes 8294404
where the time goes:
time: 215 us
  Pallas kernels  195 us (91%)
  local copies, waits for them, and re-layouts  16.6 us (8%)
  other arithmetic  2.23 us (1%)
    pallas_call x1, Pallas kernels, shards(): pl.pallas_call(kernel, out_shape=(jax.ShapeDtypeStruct((3, REAL, 128), F3...  195 us
    unnamed x9, local copies, waits for them, and re-layouts  5.82 us

commit v1 on v0

--- a/solution.py
+++ b/solution.py
@@ -28,9 +28,12 @@
 KINDS = 3
 CHUNK = OWN * KINDS * 8
 PIECE = 384
-GRAD_ROWS = 104
-PART = 32
-PARTS = 4 * GRAD_ROWS // PART
+WIDE = 4 * BLOCK
+QUARTER = BLOCK // 4
+GRAD_ROWS = 4 * QUARTER + 8
+PART = 8
+PARTS = GRAD_ROWS // PART
+EARLY = 4
 
 epsilon = 1e-05
 shrink_level = 0.05
@@ -78,11 +81,7 @@
                     else:
                         lane = 64 * part + (i if core == 0 else i - 32)
                     place[core, mode, part, i, lane] = 1.0
-    halves = np.zeros((2, 8, 128), np.float32)
-    halves[0, 0, :64] = 1.0
-    halves[0, 1, 64:] = 1.0
-    halves[1, 2, :64] = 1.0
-    halves[1, 3, 64:] = 1.0
+    ones = np.kron(np.eye(2), np.ones((64, 64)))
     bf = ml_dtypes.bfloat16
     return (
         split_table(plain, 3),
@@ -93,7 +92,7 @@
         turn,
         place.astype(bf),
         np.swapaxes(place, -1, -2).astype(bf),
-        halves,
+        ones.astype(bf),
     )
 
 
@@ -117,8 +116,25 @@
 def kernel(
     fields,
     cotangent,
-    norm,
-    weights,
+    gain,
+    shift,
+    weight1,
+    bias1,
+    weight2,
+    bias2,
+    plain_in,
+    double_in,
+    back_plain_in,
+    back_double_in,
+    lat_in,
+    turn_in,
+    place_in,
+    place_t_in,
+    ones,
+    mixed_out,
+    grad_out,
+    param_out,
+    norm_out,
     plain,
     double,
     back_plain,
@@ -127,11 +143,6 @@
     turn,
     place,
     place_t,
-    halves,
-    mixed_out,
-    grad_out,
-    param_out,
-    norm_out,
     scaled,
     cot,
     inv,
@@ -154,14 +165,19 @@
     mats_grad,
     sums_grad,
     bias,
+    norm,
+    weights,
+    stage,
     zsend,
     zrecv,
     part_send,
     part_recv,
     part_sum,
+    param_all,
     norm_send,
     norm_recv,
     io_sem,
+    table_sem,
     z_ssem,
     z_rsem,
     s_sem,
@@ -171,6 +187,7 @@
     p_rsem,
     g_ssem,
     g_rsem,
+    c_sem,
     n_ssem,
     n_rsem,
 ):
@@ -183,9 +200,10 @@
     low32 = lane % 64 < 32
     sign = jnp.where(low, 1.0, -1.0).astype(F32)
 
-    sends = (send1, send2, send3, send4)
-    recvs = (recv1, recv2, recv3, recv4)
-    mids = (mid1, mid2, mid3, mid4)
+    sends = (send1, send2, send3, send4, send4, send3)
+    recvs = (recv1, recv2, recv3, recv4, recv4, recv3)
+    mids = (mid1, mid2, mid3, mid4, mid4, mid3)
+    spans = ((0, OWN), (0, OWN), (0, EARLY), (0, EARLY), (EARLY, OWN), (EARLY, OWN))
 
     def at(dy, dx):
         return lax.rem(y + dy, 4), lax.rem(x + dx, 4)
@@ -201,7 +219,8 @@
 
     direct = [(0, 0, 2)] + [(0, d, k) for d in (1, 3, 2) for k in (0, 1)]
     direct += [(d, 0, k) for d in (1, 3, 2) for k in (0, 1)]
-    corner = [(dy, dx, k) for dy in (1, 3, 2) for dx in (1, 3, 2) for k in (0, 1)]
+    latin = [(1, 1), (3, 3), (2, 2), (1, 3), (3, 2), (2, 1), (1, 2), (3, 1), (2, 3)]
+    corner = [(dy, dx, k) for dy, dx in latin for k in (0, 1)]
 
     def corner_slot(dy, dx, k):
         return k * 9 + (dy - 1) * 3 + dx - 1
@@ -216,6 +235,10 @@
             device_id_type=MESH,
         )
 
+    def chunk(n, ref, slot):
+        first, last = spans[n]
+        return ref.at[slot, pl.ds(24 * first, 24 * (last - first))]
+
     def first_leg(n, i):
         dy, dx, k = corner[i]
         row, column = at(dy, dx)
@@ -223,7 +246,11 @@
         slot = corner_slot(dy, dx, k)
         device = index(y, column, core) if k == 0 else index(row, x, core)
         return remote(
-            sends[n].at[src_slot], mids[n].at[slot], s_sem.at[n, i], m_sem.at[n, slot], device
+            chunk(n, sends[n], src_slot),
+            chunk(n, mids[n], slot),
+            s_sem.at[n, i],
+            m_sem.at[n, slot],
+            device,
         )
 
     def second_leg(n, i):
@@ -236,8 +263,8 @@
             origin = (lax.rem(y + 4 - dy, 4), x)
             final = (y, lax.rem(x + dx, 4))
         return remote(
-            mids[n].at[slot],
-            recvs[n].at[slots(n)[1](origin[0], origin[1], core)],
+            chunk(n, mids[n], slot),
+            chunk(n, recvs[n], slots(n)[1](origin[0], origin[1], core)),
             s_sem.at[n, 18 + i],
             r_sem.at[n, index(origin[0], origin[1], core)],
             index(final[0], final[1], k),
@@ -248,24 +275,29 @@
         half = 1 - core if k == 2 else k
         row, column = at(dy, dx)
         return remote(
-            sends[n].at[slots(n)[0](row, column, half)],
-            recvs[n].at[slots(n)[1](y, x, core)],
+            chunk(n, sends[n], slots(n)[0](row, column, half)),
+            chunk(n, recvs[n], slots(n)[1](y, x, core)),
             s_sem.at[n, 36 + i],
             r_sem.at[n, me],
             index(row, column, half),
         )
 
-    def start(n):
+    def start(n, halves=(0, 1)):
         for i in range(18):
-            first_leg(n, i).start()
-        for i in range(13):
-            direct_leg(n, i).start()
-        mine = slots(n)[0](y, x, core)
-        theirs = slots(n)[1](y, x, core)
-        recvs[n][theirs] = sends[n][mine]
-
-    def forward(n):
-        for i in range(18):
+            if corner[i][2] in halves:
+                first_leg(n, i).start()
+        for i in range(1, 13):
+            if direct[i][2] in halves:
+                direct_leg(n, i).start()
+        if 1 in halves:
+            direct_leg(n, 0).start()
+            mine = slots(n)[0](y, x, core)
+            theirs = slots(n)[1](y, x, core)
+            here = pl.ds(24 * spans[n][0], 24 * (spans[n][1] - spans[n][0]))
+            recvs[n][theirs, here] = sends[n][mine, here]
+
+    def forward(n, first=0, last=18):
+        for i in range(first, last):
             first_leg(n, i).wait_recv()
             second_leg(n, i).start()
 
@@ -274,7 +306,7 @@
             origin = lax.rem(me + d, 32)
             slot = slots(n)[1](origin // 8, (origin // 2) % 4, origin % 2)
             remote(
-                sends[n].at[0], recvs[n].at[slot], s_sem.at[n, 0], r_sem.at[n, origin], origin
+                chunk(n, sends[n], 0), chunk(n, recvs[n], slot), s_sem.at[n, 0], r_sem.at[n, origin], origin
             ).wait_recv()
 
     def drain(n):
@@ -317,31 +349,28 @@
                 device_id_type=MESH,
             ).wait_recv()
 
-    def token_sums(value, which, count=3):
-        pattern = halves[which].astype(BF16)
+    lane48 = lax.broadcasted_iota(jnp.int32, (48, 8, 128), 2) % 64
+    own_lane = lane48 == lax.broadcasted_iota(jnp.int32, (48, 8, 128), 0)
+
+    def token_sums(value):
         total = None
-        for part in reversed(split(value, count)):
-            term = lax.dot_general(
-                pattern, part, (((1,), (1,)), ((), ())), preferred_element_type=F32
-            )
+        for part in reversed(split(value, 3)):
+            term = jnp.dot(part, ones[...], preferred_element_type=F32)
             total = term if total is None else total + term
         return total
 
-    def spread(rows, which):
-        return lax.dot_general(
-            rows,
-            halves[which],
-            (((0,), (0,)), ((), ())),
-            precision=lax.Precision.HIGHEST,
-            preferred_element_type=F32,
-        )
-
-    def lon_forward(load, table, pairs, out):
+    def pack(value):
+        return jnp.sum(jnp.where(own_lane, value.reshape(48, 8, 128), 0.0), axis=0)
+
+    def spread(rows):
+        return token_sums(jnp.where(own_lane, rows[None], 0.0).reshape(PIECE, 128))
+
+    def lon_forward(load, table, pairs, out, groups):
         count = 3 if pairs is SIX else 2
         flat = out.reshape(32 * CHUNK, 128)
         cos_turn, sin_turn = turn[0], turn[1]
         top = lax.broadcasted_iota(jnp.int32, (TALL, 128), 0) == 0
-        for g in range(3):
+        for g in groups:
 
             def body(step, carry, g=g):
                 h0 = step * 2
@@ -375,12 +404,12 @@
 
             lax.fori_loop(0, 4, body, 0)
 
-    def lon_inverse(source, table):
+    def lon_inverse(source, table, groups):
         flat = source.reshape(32 * CHUNK, 128)
         cos_turn, sin_turn = turn[0], turn[1]
         top = lax.broadcasted_iota(jnp.int32, (RANK, 128), 0) == 0
         top8 = lax.broadcasted_iota(jnp.int32, (8, 128), 0) == 0
-        for g in range(3):
+        for g in groups:
 
             def body(step, carry, g=g):
                 h0 = step * 2
@@ -457,19 +486,28 @@
             sums_grad[layer * 2 + mode] += jnp.sum(total.reshape(32, 8, 256), axis=0)
 
     loads = []
-    for g in range(3):
-        loads.append(
-            pltpu.make_async_copy(
-                cotangent.at[g], cot.at[pl.ds(g * STRIP, REAL)], io_sem.at[g]
+    for i, (source, target) in enumerate(((fields, scaled), (cotangent, cot))):
+        for g in range(3):
+            loads.append(
+                pltpu.make_async_copy(
+                    source.at[g], target.at[pl.ds(g * STRIP, REAL)], io_sem.at[3 * i + g]
+                )
             )
-        )
-    for g in range(3):
-        loads.append(
-            pltpu.make_async_copy(
-                fields.at[g], scaled.at[pl.ds(g * STRIP, REAL)], io_sem.at[3 + g]
-            )
-        )
-    for copy in loads:
+    pairs = (
+        (turn_in, turn),
+        (double_in, double),
+        (plain_in, plain),
+        (place_in, place),
+        (place_t_in, place_t),
+        (lat_in, lat_table),
+        (back_plain_in, back_plain),
+        (back_double_in, back_double),
+    )
+    tables = [
+        pltpu.make_async_copy(source, target, table_sem.at[i])
+        for i, (source, target) in enumerate(pairs)
+    ]
+    for copy in loads[:3]:
         copy.start()
     barrier = pltpu.get_barrier_semaphore()
     for d in range(1, 32):
@@ -483,60 +521,90 @@
     for g in range(3):
         cot[pl.ds(g * STRIP + REAL, STRIP - REAL), :] = jnp.zeros((STRIP - REAL, 128), F32)
         scaled[pl.ds(g * STRIP + REAL, STRIP - REAL), :] = jnp.zeros((STRIP - REAL, 128), F32)
+    for i, source in enumerate((gain, shift)):
+        for g in range(3):
+            value = source[:, 64 * g : 64 * g + 64]
+            norm[3 * i + g : 3 * i + g + 1, :] = jnp.concatenate([value, value], axis=1)
     for copy in loads[:3]:
         copy.wait()
-
-    def load_cot(g, h):
-        return cot[pl.ds(g * STRIP + h, PADDED, stride=8), :]
-
-    lon_forward(load_cot, double, THREE, send2)
-    pl.semaphore_wait(barrier, 34)
-    start(1)
-
-    for copy in loads[3:]:
-        copy.wait()
-    for k in range(STRIP // PIECE):
-        rows = [scaled[pl.ds(g * STRIP + k * PIECE, PIECE), :] for g in range(3)]
-        here = token_sums(rows[0] + rows[1] + rows[2], 0)
-        mean = spread(here * (1.0 / LOCAL), 0)
+    for copy in tables[:2] + loads[3:] + tables[2:]:
+        copy.start()
+
+    def stats_body(k, carry):
+        first = pl.multiple_of(k * PIECE, PIECE)
+        rows = [scaled[pl.ds(g * STRIP + first, PIECE), :] for g in range(3)]
+        here = token_sums(rows[0] + rows[1] + rows[2])
+        mean = here * (1.0 / LOCAL)
         square = None
         for value in rows:
             centred = value - mean
             square = centred * centred if square is None else square + centred * centred
-        zsend[0, :, pl.ds(k * PIECE, PIECE)] = here + token_sums(square, 1)
+        zsend[0, 0, k] = pack(here)
+        zsend[0, 1, k] = pack(token_sums(square))
+        return carry
+
+    lax.fori_loop(0, STRIP // PIECE, stats_body, 0)
+    pl.semaphore_wait(barrier, 34)
     copies = exchange(0)
+
+    def load_cot(g, h):
+        return cot[pl.ds(g * STRIP + h, PADDED, stride=8), :]
+
+    for copy in loads[3:] + tables[:2]:
+        copy.wait()
+    lon_forward(load_cot, double, THREE, send2, (0,))
     exchange_wait(0, copies)
-    row8 = lax.broadcasted_iota(jnp.int32, (8, PIECE), 0)
-    for k in range(STRIP // PIECE):
-        group = [zrecv[0, i, :, pl.ds(k * PIECE, PIECE)] for i in range(4)]
-        total = (group[0] + group[1]) + (group[2] + group[3])
-        mean = total * (1.0 / EMBED)
+
+    def norm_body(k, carry):
+        sums = [zrecv[0, i, 0, k] for i in range(4)]
+        squares = [zrecv[0, i, 1, k] for i in range(4)]
+        mean = ((sums[0] + sums[1]) + (sums[2] + sums[3])) * (1.0 / EMBED)
         apart = None
-        for value in group:
+        for value in sums:
             gap = value * (1.0 / LOCAL) - mean
             apart = gap * gap if apart is None else apart + gap * gap
-        variance = (total + pltpu.roll(apart, 2, 0) * LOCAL) * (1.0 / EMBED)
-        both = jnp.where(row8 < 2, mean, lax.rsqrt(jnp.maximum(variance, 0.0) + epsilon))
-        mean = spread(both, 0)
-        inverse = spread(both, 1)
-        inv[pl.ds(k * PIECE, PIECE), :] = inverse
+        total = (squares[0] + squares[1]) + (squares[2] + squares[3]) + apart * LOCAL
+        inverse = spread(lax.rsqrt(total * (1.0 / EMBED) + epsilon))
+        mean = spread(mean)
+        first = pl.multiple_of(k * PIECE, PIECE)
+        inv[pl.ds(first, PIECE), :] = inverse
         for g in range(3):
-            here = pl.ds(g * STRIP + k * PIECE, PIECE)
+            here = pl.ds(g * STRIP + first, PIECE)
             scaled[here, :] = (scaled[here, :] - mean) * inverse
+        return carry
+
+    lax.fori_loop(0, STRIP // PIECE, norm_body, 0)
 
     def load_normed(g, h):
         value = scaled[pl.ds(g * STRIP + h, PADDED, stride=8), :]
         return value * norm[g : g + 1] + norm[3 + g : 4 + g]
 
-    lon_forward(load_normed, plain, SIX, send1)
-    start(0)
-    forward(1)
-
+    tables[2].wait()
+    lon_forward(load_normed, plain, SIX, send1, (0, 1))
+    start(0, (0,))
+    lon_forward(load_normed, plain, SIX, send1, (2,))
+    start(0, (1,))
+    lon_forward(load_cot, double, THREE, send2, (1, 2))
+
+    for copy in tables[3:]:
+        copy.wait()
+    for layer, (weight, shifts) in enumerate(((weight1, bias1), (weight2, bias2))):
+        for part in range(2):
+            target = weights.at[layer * 2 + part]
+            target[...] = jnp.zeros((128, 128), F32)
+            for q in range(24):
+                stage[q : q + 1, :] = weight[part, pl.ds(core, 1), 384 * q : 384 * q + 384]
+            for t in range(4):
+                value = stage[:, BLOCK * t : BLOCK * t + BLOCK]
+                value = jnp.concatenate([value, jnp.zeros((24, 128 - BLOCK), F32)], axis=1)
+                target[pl.ds(t, 24, stride=4), :] = value
+            value = shifts[part, pl.ds(core, 1), :]
+            target[BLOCK : BLOCK + 1, :BLOCK] = value
     for layer in range(2):
         for mode in range(2):
             to_real, to_imag = place[core, mode, 0], place[core, mode, 1]
-            real = split(weights[layer, 0, core], 3)
-            imag = split(weights[layer, 1, core], 3)
+            real = split(weights[layer * 2], 3)
+            imag = split(weights[layer * 2 + 1], 3)
 
             def fan(parts, target):
                 total = None
@@ -559,6 +627,8 @@
             whole = lift(place_t[core, mode, 0], upper) + lift(place_t[core, mode, 1], lower)
             for i, part in enumerate(split(whole, 3)):
                 mats[layer * 2 + mode, i] = part
+    forward(0)
+    start(1)
 
     def add_bias(pieces, layer):
         first, second = bias[layer * 2], bias[layer * 2 + 1]
@@ -568,16 +638,6 @@
             pieces[2] + (first[0:1, 128:] + second[0:1, 128:]),
         ]
 
-    finish(1)
-
-    def upstream_body(r, carry):
-        out = lat_mix([piece(recv2, r, kind) for kind in range(3)], 1.0, THREE)
-        for kind in range(3):
-            put(recv2, r, kind, out[kind])
-        return carry
-
-    lax.fori_loop(0, OWN, upstream_body, 0)
-    forward(0)
     finish(0)
 
     def forward_body(r, carry):
@@ -596,16 +656,19 @@
             put(send3, r, kind, rows[kind])
         return carry
 
-    lax.fori_loop(0, OWN, forward_body, 0)
+    forward(1)
+    lax.fori_loop(0, EARLY, forward_body, 0)
     start(2)
+    lax.fori_loop(EARLY, OWN, forward_body, 0)
+    finish(1)
 
     mats_grad[...] = jnp.zeros_like(mats_grad)
     sums_grad[...] = jnp.zeros_like(sums_grad)
 
     def backward_body(r, carry):
+        upstream = lat_mix([piece(recv2, r, kind) for kind in range(3)], 1.0, THREE)
         out_grad = [
-            jnp.where(piece(shrunk, r, kind) != 0.0, piece(recv2, r, kind), 0.0)
-            for kind in range(3)
+            jnp.where(piece(shrunk, r, kind) != 0.0, upstream[kind], 0.0) for kind in range(3)
         ]
         hidden = [piece(act, r, kind) for kind in range(3)]
         mat_grad(hidden, out_grad, 1)
@@ -617,7 +680,11 @@
             put(send4, r, kind, rows[kind])
         return carry
 
-    lax.fori_loop(0, OWN, backward_body, 0)
+    lax.fori_loop(0, 2, backward_body, 0)
+    forward(2)
+    lax.fori_loop(2, EARLY, backward_body, 0)
+    start(3)
+    lax.fori_loop(EARLY, OWN, backward_body, 0)
 
     bias_row = lax.broadcasted_iota(jnp.int32, (128, 128), 0) == BLOCK
     for layer in range(2):
@@ -645,8 +712,16 @@
             imag = jnp.where(bias_row, imag_bias[0:1], imag)
             real_total = real if real_total is None else real_total + real
             imag_total = imag if imag_total is None else imag_total + imag
-        part_send[pl.ds(layer * 2 * GRAD_ROWS, GRAD_ROWS), :] = real_total[:GRAD_ROWS]
-        part_send[pl.ds((layer * 2 + 1) * GRAD_ROWS, GRAD_ROWS), :] = imag_total[:GRAD_ROWS]
+        for part, value in enumerate((real_total, imag_total)):
+            weights[layer * 2 + part] = value
+    for i in range(4):
+        columns = [
+            weights[i, pl.ds(t, QUARTER, stride=4), :][:, :BLOCK] for t in range(4)
+        ]
+        part_send[pl.ds(i * QUARTER, QUARTER), :] = jnp.concatenate(columns, axis=1)
+    row = jnp.concatenate([weights[i, BLOCK : BLOCK + 1, :][:, :BLOCK] for i in range(4)], axis=1)
+    top = lax.broadcasted_iota(jnp.int32, (8, WIDE), 0) == 0
+    part_send[pl.ds(4 * QUARTER, 8), :] = jnp.where(top, row, 0.0)
 
     def part_copy(d):
         other = lax.rem(chip + d, 16)
@@ -662,19 +737,19 @@
         other, copy = part_copy(d)
         pl.when(other < PARTS)(copy.start)
     part_recv[chip] = part_send[pl.ds(lax.rem(chip, PARTS) * PART, PART), :]
-    start(3)
-    forward(2)
+    forward(3)
+    start(4)
 
     owner = chip < PARTS
 
     def sum_copy(d):
-        other = lax.rem(me + d, 32)
-        return other, remote(
+        other = lax.rem(chip + d, 16)
+        return remote(
             part_sum,
-            param_out.at[core, pl.ds(lax.rem(chip, PARTS) * PART, PART)],
+            param_all.at[core, pl.ds(lax.rem(chip, PARTS) * PART, PART)],
             g_ssem.at[d],
-            g_rsem.at[me],
-            other,
+            g_rsem.at[chip],
+            other * 2 + core,
         )
 
     @pl.when(owner)
@@ -692,49 +767,53 @@
         for i in range(1, 16):
             total = total + part_recv[i]
         part_sum[...] = total * FACTOR
-        param_out[core, pl.ds(lax.rem(chip, PARTS) * PART, PART), :] = total * FACTOR
-        for d in range(1, 32):
-            sum_copy(d)[1].start()
-
-    finish(2)
-    lon_inverse(recv3, back_double)
-    for g in range(3):
-        here = pl.ds(g * STRIP, REAL)
-        result[here, :] = (
-            result[here, :] + scaled[here, :] * norm[g : g + 1] + norm[3 + g : 4 + g]
-        )
-    stores = []
-    for g in range(3):
-        stores.append(
-            pltpu.make_async_copy(
-                result.at[pl.ds(g * STRIP, REAL)], mixed_out.at[g], io_sem.at[g]
-            )
-        )
-        stores[-1].start()
-    forward(3)
-    for copy in stores:
-        copy.wait()
+        param_all[core, pl.ds(lax.rem(chip, PARTS) * PART, PART), :] = total * FACTOR
+        for d in range(1, 16):
+            sum_copy(d).start()
+
+    forward(4)
+    start(5)
+
+    for d in range(1, 16):
+        other = lax.rem(chip + d, 16)
+        copy = remote(
+            part_sum,
+            param_all.at[core, pl.ds(lax.rem(other, PARTS) * PART, PART)],
+            g_ssem.at[d],
+            g_rsem.at[other],
+            other * 2 + core,
+        )
+        pl.when(other < PARTS)(copy.wait_recv)
+    across = remote(
+        param_all.at[core], param_all.at[core], c_sem.at[0], c_sem.at[1], index(y, x, 1 - core)
+    )
+    across.start()
     finish(3)
-
-    lon_inverse(recv4, back_plain)
-    gains = [None] * 6
-    for k in range(STRIP // PIECE):
+    finish(4)
+
+    lon_inverse(recv4, back_plain, (0, 1, 2))
+
+    def sums_body(k, gains):
         direct_sum, cross_sum = None, None
+        gains = list(gains)
+        first = pl.multiple_of(k * PIECE, PIECE)
         for g in range(3):
-            here = pl.ds(g * STRIP + k * PIECE, PIECE)
+            here = pl.ds(g * STRIP + first, PIECE)
             normed_grad = cot[here, :] + result[here, :]
             unit = scaled[here, :]
             for slot, value in ((g, normed_grad * unit), (3 + g, normed_grad)):
-                value = jnp.sum(value.reshape(PIECE // 8, 8, 128), axis=0)
-                gains[slot] = value if gains[slot] is None else gains[slot] + value
+                gains[slot] += jnp.sum(value.reshape(PIECE // 8, 8, 128), axis=0)
             scaled_grad = normed_grad * norm[g : g + 1]
             cot[here, :] = scaled_grad
             cross = scaled_grad * unit
             direct_sum = scaled_grad if direct_sum is None else direct_sum + scaled_grad
             cross_sum = cross if cross_sum is None else cross_sum + cross
-        zsend[1, :, pl.ds(k * PIECE, PIECE)] = token_sums(direct_sum, 0) + token_sums(
-            cross_sum, 1
-        )
+        zsend[1, 0, k] = pack(token_sums(direct_sum))
+        zsend[1, 1, k] = pack(token_sums(cross_sum))
+        return tuple(gains)
+
+    zero = jnp.zeros((8, 128), F32)
+    gains = lax.fori_loop(0, STRIP // PIECE, sums_body, (zero,) * 6)
     copies = exchange(1)
     norm_rows = lax.broadcasted_iota(jnp.int32, (8, 128), 0)
     packed = jnp.zeros((8, 128), F32)
@@ -750,16 +829,23 @@
 
     for d in range(1, 32):
         norm_copy(d).start()
+    forward(5)
     exchange_wait(1, copies)
-    for k in range(STRIP // PIECE):
-        group = [zrecv[1, i, :, pl.ds(k * PIECE, PIECE)] for i in range(4)]
-        total = ((group[0] + group[1]) + (group[2] + group[3])) * (1.0 / EMBED)
-        direct_mean = spread(total, 0)
-        cross_mean = spread(total, 1)
-        inverse = inv[pl.ds(k * PIECE, PIECE), :]
+
+    def grad_body(k, carry):
+        means = []
+        for which in range(2):
+            group = [zrecv[1, i, which, k] for i in range(4)]
+            total = (group[0] + group[1]) + (group[2] + group[3])
+            means.append(spread(total * (1.0 / EMBED)))
+        first = pl.multiple_of(k * PIECE, PIECE)
+        inverse = inv[pl.ds(first, PIECE), :]
         for g in range(3):
-            here = pl.ds(g * STRIP + k * PIECE, PIECE)
-            cot[here, :] = inverse * (cot[here, :] - direct_mean - scaled[here, :] * cross_mean)
+            here = pl.ds(g * STRIP + first, PIECE)
+            cot[here, :] = inverse * (cot[here, :] - means[0] - scaled[here, :] * means[1])
+        return carry
+
+    lax.fori_loop(0, STRIP // PIECE, grad_body, 0)
     stores = []
     for g in range(3):
         stores.append(
@@ -769,6 +855,30 @@
         )
         stores[-1].start()
 
+    finish(2)
+    finish(5)
+    for g in range(3):
+        lon_inverse(recv3, back_double, (g,))
+        here = pl.ds(g * STRIP, REAL)
+        result[here, :] = (
+            result[here, :] + scaled[here, :] * norm[g : g + 1] + norm[3 + g : 4 + g]
+        )
+        stores.append(
+            pltpu.make_async_copy(
+                result.at[pl.ds(g * STRIP, REAL)], mixed_out.at[g], io_sem.at[g]
+            )
+        )
+        stores[-1].start()
+
+    remote(
+        param_all.at[1 - core],
+        param_all.at[1 - core],
+        c_sem.at[0],
+        c_sem.at[1],
+        index(y, x, 1 - core),
+    ).wait_recv()
+    across.wait_send()
+    param_out[...] = param_all[...]
     for d in range(1, 32):
         other = lax.rem(me + d, 32)
         remote(
@@ -785,24 +895,61 @@
 
     @pl.when(owner)
     def _():
-        for d in range(1, 32):
-            sum_copy(d)[1].wait_send()
-
-    for d in range(1, 32):
-        other = lax.rem(me + d, 32)
-        other_chip = other // 2
-        copy = remote(
-            part_sum,
-            param_out.at[other % 2, pl.ds(lax.rem(other_chip, PARTS) * PART, PART)],
-            g_ssem.at[d],
-            g_rsem.at[other],
-            other,
-        )
-        pl.when(other_chip < PARTS)(copy.wait_recv)
-    for n in range(4):
+        for d in range(1, 16):
+            sum_copy(d).wait_send()
+
+    for n in range(6):
         drain(n)
     for copy in stores:
         copy.wait()
+
+
+def finisher(
+    mixed,
+    grad,
+    params,
+    norms,
+    mixed_out,
+    grad_out,
+    gain_out,
+    shift_out,
+    weight1_out,
+    bias1_out,
+    weight2_out,
+    bias2_out,
+    held,
+    sem,
+):
+    loads, stores = [], []
+    for i, (source, target) in enumerate(((mixed, mixed_out), (grad, grad_out))):
+        for g in range(3):
+            for part in range(3):
+                n = 9 * i + 3 * g + part
+                here = pl.ds(part * (REAL // 3), REAL // 3)
+                there = held.at[3 * i + g, here]
+                loads.append(pltpu.make_async_copy(source.at[g, here], there, sem.at[n]))
+                stores.append(pltpu.make_async_copy(there, target.at[g, here], sem.at[18 + n]))
+                loads[-1].start()
+    for load, store in zip(loads, stores):
+        load.wait()
+        store.start()
+    gain_out[...] = jnp.concatenate([norms[g : g + 1, :64] for g in range(3)], axis=1)
+    shift_out[...] = jnp.concatenate([norms[3 + g : 4 + g, :64] for g in range(3)], axis=1)
+    for layer, (weight, shifts) in enumerate(
+        ((weight1_out, bias1_out), (weight2_out, bias2_out))
+    ):
+        for part in range(2):
+            i = layer * 2 + part
+            for half in range(2):
+                for q in range(QUARTER):
+                    row = i * QUARTER + q
+                    weight[part, half : half + 1, WIDE * q : WIDE * q + WIDE] = params[
+                        half, row : row + 1, :
+                    ]
+                row = params[half, 4 * QUARTER : 4 * QUARTER + 1, :]
+                shifts[part, half : half + 1, :] = row[:, BLOCK * i : BLOCK * i + BLOCK]
+    for store in stores:
+        store.wait()
 
 
 def shards(
@@ -814,13 +961,6 @@
     def unrows(values):
         return values.reshape(3, PAIRS, 8, 128).transpose(2, 0, 1, 3).reshape(1, 8, 3, LON * 64)
 
-    norm = jnp.concatenate([norm_gain.reshape(3, 64), norm_shift.reshape(3, 64)])
-    norm = jnp.pad(jnp.concatenate([norm, norm], axis=1), ((0, 2), (0, 0)))
-    square = (2, 2, BLOCK, BLOCK)
-    weights = jnp.stack([first_weight.reshape(square), second_weight.reshape(square)])
-    biases = jnp.stack([first_bias, second_bias])[:, :, :, None, :]
-    weights = jnp.concatenate([weights, biases], axis=3)
-    weights = jnp.pad(weights, ((0, 0),) * 3 + ((0, 128 - BLOCK - 1), (0, 128 - BLOCK)))
     tables = make_tables()
     buffer = pltpu.VMEM((32, CHUNK, 128), F32)
     middle = pltpu.VMEM((18, CHUNK, 128), F32)
@@ -828,17 +968,21 @@
     dma = pltpu.SemaphoreType.DMA
     vmem = pl.BlockSpec(memory_space=pltpu.VMEM)
     anywhere = pl.BlockSpec(memory_space=pl.ANY)
-    mixed, grad, params, norms = pl.pallas_call(
+    wholes = (
+        jax.ShapeDtypeStruct((3, REAL, 128), F32),
+        jax.ShapeDtypeStruct((3, REAL, 128), F32),
+    )
+    middles = pl.pallas_call(
         kernel,
-        out_shape=(
-            jax.ShapeDtypeStruct((3, REAL, 128), F32),
-            jax.ShapeDtypeStruct((3, REAL, 128), F32),
-            jax.ShapeDtypeStruct((2, 4 * GRAD_ROWS, 128), F32),
+        out_shape=wholes
+        + (
+            jax.ShapeDtypeStruct((2, GRAD_ROWS, WIDE), F32),
             jax.ShapeDtypeStruct((8, 128), F32),
         ),
-        in_specs=[anywhere] * 2 + [vmem] * 11,
+        in_specs=[anywhere] * 2 + [vmem] * 6 + [anywhere] * 8 + [vmem],
         out_specs=[anywhere] * 2 + [vmem] * 2,
-        scratch_shapes=[
+        scratch_shapes=[pltpu.VMEM(table.shape, table.dtype) for table in tables[:8]]
+        + [
             strips,
             strips,
             pltpu.VMEM((STRIP, 128), F32),
@@ -853,23 +997,29 @@
             pltpu.VMEM((4, 256, 256), F32),
             pltpu.VMEM((4, 8, 256), F32),
             pltpu.VMEM((4, 8, 256), F32),
-            pltpu.VMEM((2, 8, STRIP), F32),
-            pltpu.VMEM((2, 4, 8, STRIP), F32),
-            pltpu.VMEM((4 * GRAD_ROWS, 128), F32),
-            pltpu.VMEM((16, PART, 128), F32),
-            pltpu.VMEM((PART, 128), F32),
+            pltpu.VMEM((8, 128), F32),
+            pltpu.VMEM((4, 128, 128), F32),
+            pltpu.VMEM((24, 384), F32),
+            pltpu.VMEM((2, 2, STRIP // PIECE, 8, 128), F32),
+            pltpu.VMEM((2, 4, 2, STRIP // PIECE, 8, 128), F32),
+            pltpu.VMEM((GRAD_ROWS, WIDE), F32),
+            pltpu.VMEM((16, PART, WIDE), F32),
+            pltpu.VMEM((PART, WIDE), F32),
+            pltpu.VMEM((2, GRAD_ROWS, WIDE), F32),
             pltpu.VMEM((8, 128), F32),
             pltpu.VMEM((32, 8, 128), F32),
             dma((6,)),
+            dma((8,)),
             dma((2, 4)),
             dma((2, 4)),
-            dma((4, 49)),
-            dma((4, 32)),
-            dma((4, 18)),
+            dma((6, 49)),
+            dma((6, 32)),
+            dma((6, 18)),
             dma((16,)),
             dma((16,)),
-            dma((32,)),
-            dma((32,)),
+            dma((16,)),
+            dma((16,)),
+            dma((2,)),
             dma((32,)),
             dma((32,)),
         ],
@@ -880,19 +1030,35 @@
             flops=5_500_000_000, bytes_accessed=12_000_000, transcendentals=0
         ),
         name="mixer",
-    )(rows(fields), rows(cotangent), norm, weights, *tables)
-    params = params.reshape(2, 2, 2, GRAD_ROWS, 128)[..., :BLOCK].transpose(1, 2, 0, 3, 4)
-    flat = (2, 2, BLOCK * BLOCK)
-    return (
-        unrows(mixed),
-        unrows(grad),
-        norms[0:3, :64].reshape(LOCAL),
-        norms[3:6, :64].reshape(LOCAL),
-        params[0, :, :, :BLOCK].reshape(flat),
-        params[0, :, :, BLOCK],
-        params[1, :, :, :BLOCK].reshape(flat),
-        params[1, :, :, BLOCK],
+    )(
+        rows(fields),
+        rows(cotangent),
+        norm_gain.reshape(1, LOCAL),
+        norm_shift.reshape(1, LOCAL),
+        first_weight,
+        first_bias,
+        second_weight,
+        second_bias,
+        *tables,
     )
+    mixed, grad, *rest = pl.pallas_call(
+        finisher,
+        out_shape=wholes
+        + (
+            jax.ShapeDtypeStruct((1, LOCAL), F32),
+            jax.ShapeDtypeStruct((1, LOCAL), F32),
+            jax.ShapeDtypeStruct(first_weight.shape, F32),
+            jax.ShapeDtypeStruct(first_bias.shape, F32),
+            jax.ShapeDtypeStruct(second_weight.shape, F32),
+            jax.ShapeDtypeStruct(second_bias.shape, F32),
+        ),
+        in_specs=[anywhere] * 2 + [vmem] * 2,
+        out_specs=[anywhere] * 2 + [vmem] * 6,
+        scratch_shapes=[pltpu.VMEM((6, REAL, 128), F32), dma((36,))],
+        compiler_params=pltpu.CompilerParams(vmem_limit_bytes=63 * 2**20),
+        name="finisher",
+    )(*middles)
+    return (unrows(mixed), unrows(grad), rest[0].reshape(LOCAL), rest[1].reshape(LOCAL), *rest[2:])
 
 
 def solution(mesh):

time: 215 us -> 171 us (0.80)
  Pallas kernels: 195 us -> 170 us
  local copies, waits for them, and re-layouts: 16.6 us -> 0 us
  other arithmetic: 2.23 us -> 0 us
    pallas_call x1 -> x2, Pallas kernels: 195 us -> 170 us  [the longest x1 163 us: shards(): pl.pallas_call(kernel, out_shape=wholes + (jax.ShapeDtypeStruct((2, GRAD_...]
    another operation x4 -> x0, local copies, waits for them, and re-layouts: 5.83 us -> none  [the longest x2 2.18 us: shards(): jnp.stack([first_weight.reshape(square), second_weight.reshape(square)])]
    unnamed x9 -> x0, local copies, waits for them, and re-layouts: 5.82 us -> none
    reshape x4 -> x0, local copies, waits for them, and re-layouts: 2.8 us -> none  [the longest x1 0.76 us: shards(): norm_shift.reshape(3, 64)]
where the time goes in v1:
time: 171 us
  Pallas kernels  170 us (99%)
    pallas_call x1, Pallas kernels, shards(): pl.pallas_call(kernel, out_shape=wholes + (jax.ShapeDtypeStruct((2, GRAD_...  163 us
    pallas_call x1, Pallas kernels, shards(): pl.pallas_call(finisher, out_shape=wholes + (jax.ShapeDtypeStruct((1, LOC...  6.93 us

profile of v1, /device:TPU:1, one launch (start us, length us, event | category | flops | bytes accessed | tf_op | source)
XLA Modules:
  0.0 170.7 jit_solution(14860220311115673183)
XLA Ops:
  0.6 163.0 %mixer.1 = (f32[3,1800,128]{2,1,0:T(8,128)}, f32[3,1800,128]{2,1,0:T(8,128)}, f32[2,104,384]{2,1,0:T(8,128)}, f32[8,128]{1,0:T(8,128)}) custom-call(f32[3,1800,128]{2,1,0:T(8,128)} %bitcast.24, f32[3,1800,128]{2,1,0:T(8,128)} %bitcast.25, f32[1,192]{1,0:T(1,128)} %bitcast.28, f32[1,192]{1,0:T(1,128)} %bitcast.29, f32[2,2,9216]{2,1,0:T(2,128)} %weight1.1, ...), custom_call_target="tpu_custom_call" | custom-call | flops 5500000256 | bytes 12000000 | tf_op jit(solution)/shard_map/mixer/pallas_call | solution.py:975
  163.6 6.9 %finisher.1 = (f32[3,1800,128]{2,1,0:T(8,128)}, f32[3,1800,128]{2,1,0:T(8,128)}, f32[1,192]{1,0:T(1,128)}, f32[1,192]{1,0:T(1,128)}, f32[2,2,9216]{2,1,0:T(2,128...) custom-call(f32[3,1800,128]{2,1,0:T(8,128)} %get-tuple-element.20.mixed, ...), custom_call_target="tpu_custom_call" | custom-call | tf_op jit(solution)/shard_map/finisher/pallas_call | solution.py:1044

commit v2 on v1

--- a/solution.py
+++ b/solution.py
@@ -402,7 +402,7 @@
                         store(g // 2, 1, b)
                 return carry
 
-            lax.fori_loop(0, 4, body, 0)
+            lax.fori_loop(0, 4, body, 0, unroll=True)
 
     def lon_inverse(source, table, groups):
         flat = source.reshape(32 * CHUNK, 128)
@@ -443,7 +443,7 @@
                     ]
                 return carry
 
-            lax.fori_loop(0, 4, body, 0)
+            lax.fori_loop(0, 4, body, 0, unroll=True)
 
     def piece(ref, r, kind):
         return ref[:, pl.ds(pl.multiple_of(r * 24 + kind * 8, 8), 8), :].reshape(256, 128)
@@ -543,7 +543,7 @@
         zsend[0, 1, k] = pack(token_sums(square))
         return carry
 
-    lax.fori_loop(0, STRIP // PIECE, stats_body, 0)
+    lax.fori_loop(0, STRIP // PIECE, stats_body, 0, unroll=True)
     pl.semaphore_wait(barrier, 34)
     copies = exchange(0)
 
@@ -573,7 +573,7 @@
             scaled[here, :] = (scaled[here, :] - mean) * inverse
         return carry
 
-    lax.fori_loop(0, STRIP // PIECE, norm_body, 0)
+    lax.fori_loop(0, STRIP // PIECE, norm_body, 0, unroll=True)
 
     def load_normed(g, h):
         value = scaled[pl.ds(g * STRIP + h, PADDED, stride=8), :]
@@ -771,6 +771,8 @@
         for d in range(1, 16):
             sum_copy(d).start()
 
+    for n in range(3):
+        drain(n)
     forward(4)
     start(5)
 
@@ -813,7 +815,7 @@
         return tuple(gains)
 
     zero = jnp.zeros((8, 128), F32)
-    gains = lax.fori_loop(0, STRIP // PIECE, sums_body, (zero,) * 6)
+    gains = lax.fori_loop(0, STRIP // PIECE, sums_body, (zero,) * 6, unroll=True)
     copies = exchange(1)
     norm_rows = lax.broadcasted_iota(jnp.int32, (8, 128), 0)
     packed = jnp.zeros((8, 128), F32)
@@ -845,27 +847,12 @@
             cot[here, :] = inverse * (cot[here, :] - means[0] - scaled[here, :] * means[1])
         return carry
 
-    lax.fori_loop(0, STRIP // PIECE, grad_body, 0)
+    lax.fori_loop(0, STRIP // PIECE, grad_body, 0, unroll=True)
     stores = []
     for g in range(3):
         stores.append(
             pltpu.make_async_copy(
                 cot.at[pl.ds(g * STRIP, REAL)], grad_out.at[g], io_sem.at[3 + g]
-            )
-        )
-        stores[-1].start()
-
-    finish(2)
-    finish(5)
-    for g in range(3):
-        lon_inverse(recv3, back_double, (g,))
-        here = pl.ds(g * STRIP, REAL)
-        result[here, :] = (
-            result[here, :] + scaled[here, :] * norm[g : g + 1] + norm[3 + g : 4 + g]
-        )
-        stores.append(
-            pltpu.make_async_copy(
-                result.at[pl.ds(g * STRIP, REAL)], mixed_out.at[g], io_sem.at[g]
             )
         )
         stores[-1].start()
@@ -898,8 +885,24 @@
         for d in range(1, 16):
             sum_copy(d).wait_send()
 
-    for n in range(6):
-        drain(n)
+    drain(3)
+    drain(4)
+
+    finish(2)
+    finish(5)
+    for g in range(3):
+        lon_inverse(recv3, back_double, (g,))
+        here = pl.ds(g * STRIP, REAL)
+        result[here, :] = (
+            result[here, :] + scaled[here, :] * norm[g : g + 1] + norm[3 + g : 4 + g]
+        )
+        stores.append(
+            pltpu.make_async_copy(
+                result.at[pl.ds(g * STRIP, REAL)], mixed_out.at[g], io_sem.at[g]
+            )
+        )
+        stores[-1].start()
+    drain(5)
     for copy in stores:
         copy.wait()
 

time: 171 us -> 162 us (0.947)
  Pallas kernels: 170 us -> 161 us
    pallas_call x1, Pallas kernels: 163 us -> 154 us  [shards(): pl.pallas_call(kernel, out_shape=wholes + (jax.ShapeDtypeStruct((2, GRAD_...]
where the time goes in v2:
time: 162 us
  Pallas kernels  161 us (99%)
    pallas_call x1, Pallas kernels, shards(): pl.pallas_call(kernel, out_shape=wholes + (jax.ShapeDtypeStruct((2, GRAD_...  154 us
    pallas_call x1, Pallas kernels, shards(): pl.pallas_call(finisher, out_shape=wholes + (jax.ShapeDtypeStruct((1, LOC...  6.93 us

profile of v2, /device:TPU:1, one launch (start us, length us, event | category | flops | bytes accessed | tf_op | source)
XLA Modules:
  0.0 161.7 jit_solution(5818540843984282222)
XLA Ops:
  0.6 154.0 %mixer.1 = (f32[3,1800,128]{2,1,0:T(8,128)}, f32[3,1800,128]{2,1,0:T(8,128)}, f32[2,104,384]{2,1,0:T(8,128)}, f32[8,128]{1,0:T(8,128)}) custom-call(f32[3,1800,128]{2,1,0:T(8,128)} %bitcast.24, f32[3,1800,128]{2,1,0:T(8,128)} %bitcast.25, f32[1,192]{1,0:T(1,128)} %bitcast.28, f32[1,192]{1,0:T(1,128)} %bitcast.29, f32[2,2,9216]{2,1,0:T(2,128)} %weight1.1, ...), custom_call_target="tpu_custom_call" | custom-call | flops 5500000256 | bytes 12000000 | tf_op jit(solution)/shard_map/mixer/pallas_call | solution.py:978
  154.6 6.9 %finisher.1 = (f32[3,1800,128]{2,1,0:T(8,128)}, f32[3,1800,128]{2,1,0:T(8,128)}, f32[1,192]{1,0:T(1,128)}, f32[1,192]{1,0:T(1,128)}, f32[2,2,9216]{2,1,0:T(2,128...) custom-call(f32[3,1800,128]{2,1,0:T(8,128)} %get-tuple-element.20.mixed, ...), custom_call_target="tpu_custom_call" | custom-call | tf_op jit(solution)/shard_map/finisher/pallas_call | solution.py:1047

commit v3 on v2

--- a/solution.py
+++ b/solution.py
@@ -920,22 +920,16 @@
     bias1_out,
     weight2_out,
     bias2_out,
-    held,
     sem,
 ):
-    loads, stores = [], []
+    stores = []
     for i, (source, target) in enumerate(((mixed, mixed_out), (grad, grad_out))):
         for g in range(3):
             for part in range(3):
                 n = 9 * i + 3 * g + part
                 here = pl.ds(part * (REAL // 3), REAL // 3)
-                there = held.at[3 * i + g, here]
-                loads.append(pltpu.make_async_copy(source.at[g, here], there, sem.at[n]))
-                stores.append(pltpu.make_async_copy(there, target.at[g, here], sem.at[18 + n]))
-                loads[-1].start()
-    for load, store in zip(loads, stores):
-        load.wait()
-        store.start()
+                stores.append(pltpu.make_async_copy(source.at[g, here], target.at[g, here], sem.at[18 + n]))
+                stores[-1].start()
     gain_out[...] = jnp.concatenate([norms[g : g + 1, :64] for g in range(3)], axis=1)
     shift_out[...] = jnp.concatenate([norms[3 + g : 4 + g, :64] for g in range(3)], axis=1)
     for layer, (weight, shifts) in enumerate(
@@ -975,12 +969,13 @@
         jax.ShapeDtypeStruct((3, REAL, 128), F32),
         jax.ShapeDtypeStruct((3, REAL, 128), F32),
     )
+    inside = (pltpu.VMEM((3, REAL, 128), F32),) * 2
     middles = pl.pallas_call(
         kernel,
-        out_shape=wholes
+        out_shape=inside
         + (
-            jax.ShapeDtypeStruct((2, GRAD_ROWS, WIDE), F32),
-            jax.ShapeDtypeStruct((8, 128), F32),
+            pltpu.VMEM((2, GRAD_ROWS, WIDE), F32),
+            pltpu.VMEM((8, 128), F32),
         ),
         in_specs=[anywhere] * 2 + [vmem] * 6 + [anywhere] * 8 + [vmem],
         out_specs=[anywhere] * 2 + [vmem] * 2,
@@ -1027,7 +1022,7 @@
             dma((32,)),
         ],
         compiler_params=pltpu.CompilerParams(
-            collective_id=1, has_side_effects=True, vmem_limit_bytes=63 * 2**20
+            collective_id=1, has_side_effects=True, vmem_limit_bytes=55 * 2**20
         ),
         cost_estimate=pl.CostEstimate(
             flops=5_500_000_000, bytes_accessed=12_000_000, transcendentals=0
@@ -1057,8 +1052,8 @@
         ),
         in_specs=[anywhere] * 2 + [vmem] * 2,
         out_specs=[anywhere] * 2 + [vmem] * 6,
-        scratch_shapes=[pltpu.VMEM((6, REAL, 128), F32), dma((36,))],
-        compiler_params=pltpu.CompilerParams(vmem_limit_bytes=63 * 2**20),
+        scratch_shapes=[dma((36,))],
+        compiler_params=pltpu.CompilerParams(vmem_limit_bytes=4 * 2**20),
         name="finisher",
     )(*middles)
     return (unrows(mixed), unrows(grad), rest[0].reshape(LOCAL), rest[1].reshape(LOCAL), *rest[2:])

time: 162 us -> 158 us (0.975)
  Pallas kernels: 161 us -> 157 us
    pallas_call x1, Pallas kernels: 6.93 us -> 3.56 us  [shards(): pl.pallas_call(finisher, out_shape=wholes + (jax.ShapeDtypeStruct((1, LOC...]
where the time goes in v3:
time: 158 us
  Pallas kernels  157 us (99%)
    pallas_call x1, Pallas kernels, shards(): pl.pallas_call(kernel, out_shape=inside + (pltpu.VMEM((2, GRAD_ROWS, WIDE...  154 us
    pallas_call x1, Pallas kernels, shards(): pl.pallas_call(finisher, out_shape=wholes + (jax.ShapeDtypeStruct((1, LOC...  3.56 us

profile of v3, /device:TPU:1, one launch (start us, length us, event | category | flops | bytes accessed | tf_op | source)
XLA Modules:
  0.0 158.0 jit_solution(8186329173712571980)
XLA Ops:
  0.6 153.6 %mixer.1 = (f32[3,1800,128]{2,1,0:T(8,128)S(1)}, f32[3,1800,128]{2,1,0:T(8,128)S(1)}, f32[2,104,384]{2,1,0:T(8,128)S(1)}, f32[8,128]{1,0:T(8,128)S(1)}) custom-call(f32[3,1800,128]{2,1,0:T(8,128)} %bitcast.24, f32[3,1800,128]{2,1,0:T(8,128)} %bitcast.25, f32[1,192]{1,0:T(1,128)} %bitcast.28, f32[1,192]{1,0:T(1,128)} %bitcast.29, f32[2,2,9216]{2,1,0:T(2,128)} %weight1.1, ...), custom_call_target="tpu_custom_call" | custom-call | flops 5500000256 | bytes 12000000 | tf_op jit(solution)/shard_map/mixer/pallas_call | solution.py:973
  154.3 3.6 %finisher.1 = (f32[3,1800,128]{2,1,0:T(8,128)}, f32[3,1800,128]{2,1,0:T(8,128)}, f32[1,192]{1,0:T(1,128)}, f32[1,192]{1,0:T(1,128)}, f32[2,2,9216]{2,1,0:T(2,128...) custom-call(f32[3,1800,128]{2,1,0:T(8,128)S(1)} %get-tuple-element.20.mixed, ...), custom_call_target="tpu_custom_call" | custom-call | tf_op jit(solution)/shard_map/finisher/pallas_call | solution.py:1042
